TPU v7x, 32 devices: a whole 2x2x4 slice. The times are simulated.
32 devices in a mesh: section: 2 (over core), seq: 2 (over x), table: 8 (over z, y).
Axes of the slice: x: 2, y: 2, z: 4, core: 2. Of those that a mesh axis runs over, the one named last changes fastest.
Arguments:
- table_slab: bfloat16 [8192, 512], P('table'), may hold values from -6 to 6
- request_rows: int32 [16, 512], P(('seq', 'table')), may hold values from 0 to 1023
- owner_counts: int32 [16, 8], P(('seq', 'table')), may hold values from 1 to 64, as said below
- item_slots: int32 [16, 1024], P(('seq', 'table')), may hold values from 0 to 511, as said below
- regroup_counts: int32 [8, 2, 2], P('table'), may hold values from 256 to 768, as said below
- history_lengths: int32 [64, 8], P(('seq', 'table')), may hold values from 1 to 128, 256 in all within a row
- w_proj: bfloat16 [2, 512, 2048], P('section'), may hold values from -0.25 to 0.25
- bias_proj: float32 [2, 2048], P('section'), may hold values from -3 to 3
- gain_in: float32 [2, 512], P('section'), may hold values from 0.5 to 1.5
- gain_mid: float32 [2, 512], P('section'), may hold values from 0.5 to 1.5
- rel_bias: float32 [2, 4, 128], P('section'), may hold values from -4 to 4
- w_out: bfloat16 [2, 512, 512], P('section'), may hold values from -0.25 to 0.25
Outputs:
- states: bfloat16 [2, 16384, 512], P('section', ('seq', 'table'))
Inputs may be any that keep to these rules, and one draw needn't show every extreme that they name: `owner_counts`: each block's requests are listed owner by owner; in every set of blocks with one seq index, some owner receives 64 requests from each of them. `item_slots`: every slot lies below the sum of its block's owner_counts. `regroup_counts`: for every table index, each source's and each destination's counts sum to 1024; each source's events are ordered by destination, and a destination lays its events out source after source; every row and every column reaches 768.
All inputs are finite; a program needn't handle non-finite values.
Results may differ from a plain program's by a relative error of at most 0.0064.
Values may be sent and summed in bfloat16 or wider, within the bound.
A program may use at most 64 MiB of HBM per device.

v0:
```python
import jax
import jax.numpy as jnp
from jax import lax
from jax.sharding import PartitionSpec as P

HEADS = 4
MB_TOK = 256
CAP = 64


def shifted(shard, axis, by):
    peers = lax.axis_size(axis)
    pairs = [(i, i + by) for i in range(peers) if 0 <= i + by < peers]
    return lax.ppermute(shard, axis, pairs)


def layer_norm(values, gain_row):
    center = values - jnp.mean(values, axis=-1, keepdims=True)
    spread = jnp.mean(center * center, axis=-1, keepdims=True)
    return center * lax.rsqrt(spread + 1e-05) * gain_row


def user_mask(lengths, row_count):
    limits = jnp.cumsum(lengths)
    places = jnp.arange(row_count, dtype=jnp.int32)
    owners = jnp.sum((places[:, None] >= limits[None, :]).astype(jnp.int32), axis=1)
    return (owners[:, None] == owners[None, :]) & (places[None, :] <= places[:, None])


def bias_grid(rel_table, row_count):
    head_count, span = rel_table.shape
    left_fill = jnp.broadcast_to(rel_table[:, :1], (head_count, row_count - 1))
    right_fill = jnp.broadcast_to(rel_table[:, span - 1 :], (head_count, row_count - span))
    widened = jnp.concatenate([left_fill, rel_table, right_fill], axis=1)
    flipped = widened[:, ::-1]
    tiled = jnp.tile(flipped, (1, row_count + 1))
    stride = 2 * row_count - 2
    window = tiled[:, row_count - 1 : row_count - 1 + row_count * stride]
    return window.reshape(head_count, row_count, stride)[:, :, :row_count]


def hstu_block(block_rows, lengths, layer_weights):
    w_proj, bias_proj, gain_in, gain_mid, grid, w_out = layer_weights
    row_count, model_width = block_rows.shape
    head_size = model_width // HEADS
    residual = block_rows.astype(jnp.float32)
    normed = layer_norm(residual, gain_in).astype(jnp.bfloat16)
    projected = jnp.dot(normed, w_proj, preferred_element_type=jnp.float32) + bias_proj
    four_parts = jax.nn.silu(projected).astype(jnp.bfloat16)
    gate_part = four_parts[:, :model_width]
    value_part = four_parts[:, model_width : 2 * model_width].reshape(row_count, HEADS, head_size)
    query_part = four_parts[:, 2 * model_width : 3 * model_width].reshape(
        row_count, HEADS, head_size
    )
    key_part = four_parts[:, 3 * model_width :].reshape(row_count, HEADS, head_size)
    scores = jnp.einsum("ihd,jhd->hij", query_part, key_part, preferred_element_type=jnp.float32)
    scores = scores * head_size ** (-0.5) + grid
    masked = user_mask(lengths, row_count)[None]
    attend_weights = jnp.where(masked, jax.nn.silu(scores), jnp.zeros_like(scores)).astype(
        jnp.bfloat16
    )
    attended = jnp.einsum(
        "hij,jhd->ihd", attend_weights, value_part, preferred_element_type=jnp.float32
    )
    attended = attended.reshape(row_count, model_width)
    gated = (layer_norm(attended, gain_mid) * gate_part.astype(jnp.float32)).astype(jnp.bfloat16)
    return (residual + jnp.dot(gated, w_out, preferred_element_type=jnp.float32)).astype(
        jnp.bfloat16
    )


def fetch_rows(slab_part, request_rows, owner_counts, item_slots):
    row_counts = owner_counts[0]
    owner_total = row_counts.shape[0]
    limits = jnp.cumsum(row_counts)
    firsts = limits - row_counts
    offsets = jnp.arange(CAP, dtype=jnp.int32)
    listed = request_rows[0]
    wanted = jnp.minimum(firsts[:, None] + offsets[None, :], listed.shape[0] - 1)
    valid_slot = offsets[None, :] < row_counts[:, None]
    asked_rows = jnp.where(valid_slot, listed[wanted], 0)
    looked_up = slab_part[
        lax.all_to_all(asked_rows, "table", split_axis=0, concat_axis=0, tiled=True)
    ]
    fetched = lax.all_to_all(looked_up, "table", split_axis=0, concat_axis=0, tiled=True)
    slot_list = item_slots[0]
    owner_of = jnp.sum((slot_list[:, None] >= limits[None, :]).astype(jnp.int32), axis=1)
    flat_index = owner_of * CAP + slot_list - firsts[owner_of]
    return fetched.reshape(owner_total * CAP, -1)[flat_index]


def regroup_rows(event_rows, regroup_counts):
    send_plan = regroup_counts[0]
    peer_count = send_plan.shape[0]
    token_count = event_rows.shape[0]
    capacity = token_count // peer_count + token_count // (2 * peer_count)
    seq_index = lax.axis_index("seq")
    sent_counts = send_plan[seq_index]
    send_start = jnp.cumsum(sent_counts) - sent_counts
    take_index = jnp.minimum(
        send_start[:, None] + jnp.arange(capacity, dtype=jnp.int32)[None, :], token_count - 1
    )
    outgoing = event_rows[take_index]
    incoming = lax.all_to_all(outgoing, "seq", split_axis=0, concat_axis=0, tiled=True)
    got_counts = send_plan[:, seq_index]
    recv_last = jnp.cumsum(got_counts)
    recv_first = recv_last - got_counts
    places = jnp.arange(token_count, dtype=jnp.int32)
    sources = jnp.sum((places[:, None] >= recv_last[None, :]).astype(jnp.int32), axis=1)
    pick_index = sources * capacity + places - recv_first[sources]
    return incoming.reshape(peer_count * capacity, -1)[pick_index]


def shards(
    table_slab,
    request_rows,
    owner_counts,
    item_slots,
    regroup_counts,
    history_lengths,
    w_proj,
    bias_proj,
    gain_in,
    gain_mid,
    rel_bias,
    w_out,
):
    full_width = table_slab.shape[1]
    section_index = lax.axis_index("section")
    first_section = section_index == 0
    events = regroup_rows(
        fetch_rows(table_slab, request_rows, owner_counts, item_slots), regroup_counts
    )
    micro_count = events.shape[0] // MB_TOK
    blocks = events.reshape(micro_count, MB_TOK, full_width)
    layer_weights = (
        w_proj[0],
        bias_proj[0],
        gain_in[0],
        gain_mid[0],
        bias_grid(rel_bias[0], MB_TOK),
        w_out[0],
    )
    outputs = []
    carried = blocks[0]
    for moment in range(micro_count + 1):
        front_pick = min(moment, micro_count - 1)
        back_pick = max(moment - 1, 0)
        if moment == 0:
            source_rows = blocks[0]
        else:
            received = shifted(carried, "section", 1)
            source_rows = jnp.where(first_section, blocks[front_pick], received)
        lengths_now = jnp.where(
            first_section, history_lengths[front_pick], history_lengths[back_pick]
        )
        carried = hstu_block(source_rows, lengths_now, layer_weights)
        outputs.append(carried)
    result = jnp.where(first_section, jnp.stack(outputs[:micro_count]), jnp.stack(outputs[1:]))
    return result.reshape(1, micro_count * MB_TOK, full_width)


def solution(mesh):
    in_specs = (
        P("table", None),
        P(("seq", "table"), None),
        P(("seq", "table"), None),
        P(("seq", "table"), None),
        P("table", None, None),
        P(("seq", "table"), None),
        P("section", None, None),
        P("section", None),
        P("section", None),
        P("section", None),
        P("section", None, None),
        P("section", None, None),
    )
    out_specs = P("section", ("seq", "table"), None)
    return jax.shard_map(shards, mesh=mesh, in_specs=in_specs, out_specs=out_specs, check_vma=False)
```

profile of v0, /device:TPU:0, one launch (start us, length us, event | category | flops | bytes accessed | tf_op | source)
XLA Modules:
  0.0 156.6 jit_solution(7923768225343080703)
XLA Ops:
  1.9 3.5 %gather_fusion = s32[512]{0:T(512)S(1)} fusion(s32[512]{0:T(512)S(1)} %bitcast.238, s32[1024]{0:T(1024)S(1)} %pad_clamp_fusion.2), kind=kCustom, calls=%fused_computation | custom fusion | bytes 6144 | tf_op jit(solution)/shard_map/gather | solution.py:81
  6.1 7.3 %all-to-all-start = ((s32[8,1,64]{2,1,0:T(1,128)}), s32[8,1,64]{2,1,0:T(1,128)S(1)}, u32[]{:S(2)}, u32[]{:S(2)}) async-start(s32[8,1,64]{2,1,0:T(1,128)} %compare_select_fusion.12), calls=%async_computation | async-start | bytes 8192 | tf_op jit(solution)/shard_map/all_to_all | solution.py:83
  15.5 4.3 %all-to-all-done = s32[8,1,64]{2,1,0:T(1,128)S(1)} async-done(((s32[8,1,64]{2,1,0:T(1,128)}), s32[8,1,64]{2,1,0:T(1,128)S(1)}, u32[]{:S(2)}, u32[]{:S(2)}) %all-to-all-start) | async-done | bytes 2080 | tf_op jit(solution)/shard_map/all_to_all | solution.py:83
  19.9 2.6 %gather_fusion.1 = bf16[512,512]{1,0:T(8,128)(2,1)} fusion(bf16[1024,512]{1,0:T(8,128)(2,1)S(1)} %copy-done.3, s32[1024]{0:T(1024)S(1)} %pad_clamp_fusion.1), kind=kCustom, calls=%fused_computation.1 | custom fusion | bytes 1050624 | tf_op jit(solution)/shard_map/gather | solution.py:82
  22.5 3.5 %all-to-all-start.1 = ((bf16[8,64,512]{2,1,0:T(8,128)(2,1)}), bf16[8,64,512]{2,1,0:T(8,128)(2,1)S(1)}, u32[]{:S(2)}, u32[]{:S(2)}) async-start(bf16[8,64,512]{2,1,0:T(8,128)(2,1)} %bitcast.246), calls=%async_computation.1 | async-start | bytes 1048576 | tf_op jit(solution)/shard_map/all_to_all | solution.py:85
  28.3 5.2 %tile.10 = f32[4,131327]{1,0:T(4,128)} reshape(f32[4,257,511]{2,1,0:T(8,128)} %tile.4) | data formatting | bytes 4202464 | tf_op jit(solution)/shard_map/tile | solution.py:36
  33.5 4.1 %slice.165 = f32[4,130560]{1,0:T(4,128)} slice(f32[4,131327]{1,0:T(4,128)} %tile.10), slice={[0:4], [255:130815]} | slice | bytes 4177920 | tf_op jit(solution)/shard_map/slice | solution.py:38
  37.6 5.4 %reshape.934 = f32[4,256,510]{2,1,0:T(8,128)} reshape(f32[4,130560]{1,0:T(4,128)} %slice.165) | data formatting | bytes 4177920 | tf_op jit(solution)/shard_map/reshape | solution.py:39
  43.2 4.3 %compare_select_fusion.6 = s32[1024,1]{0,1:T(1,128)S(1)} fusion(s32[]{:T(128)} %bitcast.11, s32[]{:T(128)} %bitcast.12, s32[]{:T(128)} %bitcast.13, s32[]{:T(128)} %bitcast.14, s32[]{:T(128)} %bitcast.15, s32[]{:T(128)} %bitcast.17, s32[]{:T(128)} %bitcast.16, s32[1024,1]{0,1:T(1,128)S(1)} %bitcast.255), kind=kLoop, calls=%fused_computation.221 | loop fusion | flops 15360 | bytes 8220 | tf_op jit(solution)/shard_map/gather | solution.py:88
  49.1 5.1 %gather_fusion.2 = bf16[1024,512]{1,0:T(8,128)(2,1)S(1)} fusion(bf16[512,512]{1,0:T(8,128)(2,1)} %bitcast.239, s32[1024]{0:T(1024)S(1)} %broadcast_clamp_fusion.1), kind=kCustom, calls=%fused_computation.2 | custom fusion | bytes 2101248 | tf_op jit(solution)/shard_map/gather | solution.py:89
  54.2 5.4 %gather_fusion.3 = bf16[1536,512]{1,0:T(8,128)(2,1)} fusion(bf16[1024,512]{1,0:T(8,128)(2,1)S(1)} %gather_fusion.2, s32[2048]{0:T(1024)S(1)} %pad_clamp_fusion), kind=kCustom, calls=%fused_computation.3 | custom fusion | bytes 3151872 | tf_op jit(solution)/shard_map/gather | solution.py:103
  59.6 4.8 %all-to-all-start.2 = ((bf16[2,768,512]{2,1,0:T(8,128)(2,1)}), bf16[2,768,512]{2,1,0:T(8,128)(2,1)}, u32[]{:S(2)}, u32[]{:S(2)}) async-start(bf16[2,768,512]{2,1,0:T(8,128)(2,1)} %bitcast.240), calls=%async_computation.2 | async-start | bytes 3145728 | tf_op jit(solution)/shard_map/all_to_all | solution.py:104
  66.4 16.0 %all-to-all-done.2 = bf16[2,768,512]{2,1,0:T(8,128)(2,1)} async-done(((bf16[2,768,512]{2,1,0:T(8,128)(2,1)}), bf16[2,768,512]{2,1,0:T(8,128)(2,1)}, u32[]{:S(2)}, u32[]{:S(2)}) %all-to-all-start.2) | async-done | bytes 1572896 | tf_op jit(solution)/shard_map/all_to_all | solution.py:104
  82.4 5.6 %gather_fusion.4 = bf16[1024,512]{1,0:T(8,128)(2,1)S(1)} fusion(bf16[1536,512]{1,0:T(8,128)(2,1)} %bitcast.25, s32[1024]{0:T(1024)S(1)} %broadcast_clamp_fusion), kind=kCustom, calls=%fused_computation.4 | custom fusion | bytes 2101248 | tf_op jit(solution)/shard_map/gather | solution.py:111
  91.4 2.2 %fusion.206 = (f32[256]{0:T(256)S(1)}, f32[4,128,256]{2,1,0:T(8,128)S(1)}) fusion(bf16[256,4,128]{0,2,1:T(8,128)(2,1)} %bitcast.250, f32[4,256,510]{2,1,0:T(8,128)} %reshape.934, pred[256,256]{1,0:T(8,128)(4,1)S(1)} %fusion.173, bf16[32,4,8,128]{3,2,1,0:T(8,128)(2,1)} %get-tuple-element.28, bf16[32,4,8,128]{3,2,1,0:T(8,128)(2,1)} %get-tuple-element.27), kind=kOutput, calls=%fused_computation.305 | convolution fusion | flops 136445696 | bytes 2425856 | tf_op jit(solution)/shard_map/hij,jhd->ihd/dot_general | solution.py:62
  103.0 2.8 %fusion.211 = (f32[256]{0:T(256)S(1)}, f32[4,128,256]{2,1,0:T(8,128)}) fusion(bf16[256,4,128]{0,2,1:T(8,128)(2,1)S(1)} %bitcast.251, f32[4,256,510]{2,1,0:T(8,128)} %reshape.934, pred[256,256]{1,0:T(8,128)(4,1)S(1)} %fusion.172, bf16[32,4,8,128]{3,2,1,0:T(8,128)(2,1)} %get-tuple-element.25, bf16[32,4,8,128]{3,2,1,0:T(8,128)(2,1)} %get-tuple-element.24), kind=kOutput, calls=%fused_computation.306 | convolution fusion | flops 136445696 | bytes 2425856 | tf_op jit(solution)/shard_map/hij,jhd->ihd/dot_general | solution.py:62
  108.2 2.0 %fusion.21 = bf16[256,512]{1,0:T(8,128)(2,1)} fusion(bf16[256,512]{1,0:T(8,128)(2,1)S(1)} %get-tuple-element.14, bf16[1,512,512]{2,1,0:T(8,128)(2,1)S(1)} %copy-done.4, f32[256,512]{1,0:T(8,128)S(1)} %copy.76, bf16[256,2048]{1,0:T(8,128)(2,1)} %copy-done.9, f32[256]{0:T(256)S(1)} %add_rsqrt_fusion.6, f32[256]{0:T(256)S(1)} %broadcast_multiply_fusion.6, ...), kind=kOutput, calls=%fused_computation.36 | convolution fusion | flops 135397376 | bytes 1839104 | tf_op jit(solution)/shard_map/dot_general | solution.py:67
  110.2 2.3 %collective-permute-start.1 = (bf16[256,512]{1,0:T(8,128)(2,1)}, bf16[256,512]{1,0:T(8,128)(2,1)S(1)}, u32[]{:S(2)}, u32[]{:S(2)}) collective-permute-start(bf16[256,512]{1,0:T(8,128)(2,1)} %fusion.21), channel_id=1, source_target_pairs={{0,16},{1,17},{2,18},{3,19},{4,20},{5,21},{6,22},{7,23},{8,24},{9,... | collective-permute-start | bytes 786440 | tf_op jit(solution)/shard_map/ppermute | solution.py:14
  118.1 2.8 %fusion.216 = (f32[256]{0:T(256)S(1)}, f32[4,128,256]{2,1,0:T(8,128)}) fusion(bf16[256,4,128]{0,2,1:T(8,128)(2,1)S(1)} %bitcast.252, f32[4,256,510]{2,1,0:T(8,128)} %reshape.934, pred[256,256]{1,0:T(8,128)(4,1)S(1)} %fusion.171, bf16[32,4,8,128]{3,2,1,0:T(8,128)(2,1)} %get-tuple-element.22, bf16[32,4,8,128]{3,2,1,0:T(8,128)(2,1)} %get-tuple-element.21), kind=kOutput, calls=%fused_computation.307 | convolution fusion | flops 136445696 | bytes 2425856 | tf_op jit(solution)/shard_map/hij,jhd->ihd/dot_general | solution.py:62
  125.3 2.3 %collective-permute-start.2 = (bf16[256,512]{1,0:T(8,128)(2,1)}, bf16[256,512]{1,0:T(8,128)(2,1)S(1)}, u32[]{:S(2)}, u32[]{:S(2)}) collective-permute-start(bf16[256,512]{1,0:T(8,128)(2,1)} %fusion.22), channel_id=1, source_target_pairs={{0,16},{1,17},{2,18},{3,19},{4,20},{5,21},{6,22},{7,23},{8,24},{9,... | collective-permute-start | bytes 786440 | tf_op jit(solution)/shard_map/ppermute | solution.py:14
  133.2 2.8 %fusion.221 = (f32[256]{0:T(256)S(1)}, f32[4,128,256]{2,1,0:T(8,128)}) fusion(bf16[256,4,128]{0,2,1:T(8,128)(2,1)S(1)} %bitcast.253, f32[4,256,510]{2,1,0:T(8,128)} %reshape.934, pred[256,256]{1,0:T(8,128)(4,1)S(1)} %fusion.170, bf16[32,4,8,128]{3,2,1,0:T(8,128)(2,1)} %get-tuple-element.19, bf16[32,4,8,128]{3,2,1,0:T(8,128)(2,1)} %get-tuple-element.18), kind=kOutput, calls=%fused_computation.308 | convolution fusion | flops 136445696 | bytes 2425856 | tf_op jit(solution)/shard_map/hij,jhd->ihd/dot_general | solution.py:62
  139.8 2.5 %collective-permute-start.3 = (bf16[256,512]{1,0:T(8,128)(2,1)S(1)}, bf16[256,512]{1,0:T(8,128)(2,1)S(1)}, u32[]{:S(2)}, u32[]{:S(2)}) collective-permute-start(bf16[256,512]{1,0:T(8,128)(2,1)S(1)} %fusion.23), channel_id=1, source_target_pairs={{0,16},{1,17},{2,18},{3,19},{4,20},{5,21},{6,22},{7,23},{8,24},{9,... | collective-permute-start | bytes 786440 | tf_op jit(solution)/shard_map/ppermute | solution.py:14
  147.5 2.8 %fusion.226 = (f32[256]{0:T(256)S(1)}, f32[4,128,256]{2,1,0:T(8,128)}) fusion(bf16[256,4,128]{0,2,1:T(8,128)(2,1)S(1)} %bitcast.249, f32[4,256,510]{2,1,0:T(8,128)} %reshape.934, pred[256,256]{1,0:T(8,128)(4,1)S(1)} %fusion.169, bf16[32,4,8,128]{3,2,1,0:T(8,128)(2,1)} %get-tuple-element.16, bf16[32,4,8,128]{3,2,1,0:T(8,128)(2,1)} %get-tuple-element.15), kind=kOutput, calls=%fused_computation.309 | convolution fusion | flops 136445696 | bytes 2425856 | tf_op jit(solution)/shard_map/hij,jhd->ihd/dot_general | solution.py:62
  154.2 2.5 %maximum_select_fusion = bf16[4,256,512]{2,1,0:T(8,128)(2,1)} fusion(bf16[1,256,512]{2,1,0:T(8,128)(2,1)S(1)} %bitcast.247, bf16[1,256,512]{2,1,0:T(8,128)(2,1)} %bitcast.54, bf16[1,256,512]{2,1,0:T(8,128)(2,1)} %bitcast.48, bf16[1,256,512]{2,1,0:T(8,128)(2,1)S(1)} %bitcast.248, bf16[1,256,512]{2,1,0:T(8,128)(2,1)S(1)} %fusion.25, pred[]{:T(512)S(6)} %eq.88), kind=kLoop, calls=%fused_computation.41 | loop fusion | flops 3670016 | bytes 2359297 | tf_op jit(solution)/shard_map/jit(_where)/select_n | solution.py:159
  (163 shorter events, 53.7 us)
Async XLA Ops:
  0.0 88.4 %copy-start = (bf16[1,512,2048]{2,1,0:T(8,128)(2,1)S(1)}, bf16[1,512,2048]{2,1,0:T(8,128)(2,1)}, u32[]{:S(2)}) copy-start(bf16[1,512,2048]{2,1,0:T(8,128)(2,1)} %param.18) | copy-start | bytes 6291460
  0.0 1.8 %copy-start.1 = (s32[1,512]{1,0:T(1,128)S(1)}, s32[1,512]{1,0:T(1,128)}, u32[]{:S(2)}) copy-start(s32[1,512]{1,0:T(1,128)} %param.13) | copy-start | bytes 6148
  1.8 3.7 %copy-start.20 = (s32[1,8]{1,0:T(1,128)S(1)}, s32[1,8]{1,0:T(1,128)}, u32[]{:S(2)}) copy-start(s32[1,8]{1,0:T(1,128)} %param.14) | copy-start | bytes 100
  1.8 12.3 %copy-start.18 = (s32[1,2,2]{2,1,0:T(2,128)S(1)}, s32[1,2,2]{2,1,0:T(2,128)}, u32[]{:S(2)}) copy-start(s32[1,2,2]{2,1,0:T(2,128)} %param.16) | copy-start | bytes 52
  1.8 12.5 %copy-start.17 = (s32[1,1024]{1,0:T(1,128)S(1)}, s32[1,1024]{1,0:T(1,128)}, u32[]{:S(2)}) copy-start(s32[1,1024]{1,0:T(1,128)} %param.15) | copy-start | bytes 12292
  1.9 13.1 %copy-start.19 = (s32[4,8]{1,0:T(4,128)S(1)}, s32[4,8]{1,0:T(4,128)}, u32[]{:S(2)}) copy-start(s32[4,8]{1,0:T(4,128)} %param.17) | copy-start | bytes 388
  1.9 13.4 %copy-start.16 = (f32[1,4,128]{2,1,0:T(4,128)S(1)}, f32[1,4,128]{2,1,0:T(4,128)}, u32[]{:S(2)}) copy-start(f32[1,4,128]{2,1,0:T(4,128)} %param.22) | copy-start | bytes 6148
  1.9 18.0 %copy-start.3 = (bf16[1024,512]{1,0:T(8,128)(2,1)S(1)}, bf16[1024,512]{1,0:T(8,128)(2,1)}, u32[]{:S(2)}) copy-start(bf16[1024,512]{1,0:T(8,128)(2,1)} %param.12) | copy-start | bytes 3145732
  6.1 13.7 %all-to-all-start = ((s32[8,1,64]{2,1,0:T(1,128)}), s32[8,1,64]{2,1,0:T(1,128)S(1)}, u32[]{:S(2)}, u32[]{:S(2)}) async-start(s32[8,1,64]{2,1,0:T(1,128)} %compare_select_fusion.12), calls=%async_computation | async-start | bytes 8192 | tf_op jit(solution)/shard_map/all_to_all | solution.py:83
  22.5 25.7 %all-to-all-start.1 = ((bf16[8,64,512]{2,1,0:T(8,128)(2,1)}), bf16[8,64,512]{2,1,0:T(8,128)(2,1)S(1)}, u32[]{:S(2)}, u32[]{:S(2)}) async-start(bf16[8,64,512]{2,1,0:T(8,128)(2,1)} %bitcast.246), calls=%async_computation.1 | async-start | bytes 1048576 | tf_op jit(solution)/shard_map/all_to_all | solution.py:85
  59.6 22.8 %all-to-all-start.2 = ((bf16[2,768,512]{2,1,0:T(8,128)(2,1)}), bf16[2,768,512]{2,1,0:T(8,128)(2,1)}, u32[]{:S(2)}, u32[]{:S(2)}) async-start(bf16[2,768,512]{2,1,0:T(8,128)(2,1)} %bitcast.240), calls=%async_computation.2 | async-start | bytes 3145728 | tf_op jit(solution)/shard_map/all_to_all | solution.py:104
  82.4 6.0 %copy-start.21 = (f32[1,2048]{1,0:T(1,128)S(1)}, f32[1,2048]{1,0:T(1,128)}, u32[]{:S(2)}) copy-start(f32[1,2048]{1,0:T(1,128)} %param.19) | copy-start | bytes 24580
  82.4 6.0 %copy-start.22 = (f32[1,512]{1,0:T(1,128)S(1)}, f32[1,512]{1,0:T(1,128)}, u32[]{:S(2)}) copy-start(f32[1,512]{1,0:T(1,128)} %param.20) | copy-start | bytes 6148
  88.0 1.3 copy-start.5
  91.4 3.3 %copy-start.4 = (bf16[1,512,512]{2,1,0:T(8,128)(2,1)S(1)}, bf16[1,512,512]{2,1,0:T(8,128)(2,1)}, u32[]{:S(2)}) copy-start(bf16[1,512,512]{2,1,0:T(8,128)(2,1)} %param.23) | copy-start | bytes 1572868
  91.4 3.3 %copy-start.15 = (f32[1,512]{1,0:T(1,128)S(1)}, f32[1,512]{1,0:T(1,128)}, u32[]{:S(2)}) copy-start(f32[1,512]{1,0:T(1,128)} %param.21) | copy-start | bytes 6148
  96.2 1.7 %copy-start.13 = (bf16[256,512]{1,0:T(8,128)(2,1)}, bf16[256,512]{1,0:T(8,128)(2,1)S(1)}, u32[]{:S(2)}) copy-start(bf16[256,512]{1,0:T(8,128)(2,1)S(1)} %fusion.20) | copy-start | bytes 786436
  96.3 2.4 %collective-permute-start = (bf16[256,512]{1,0:T(8,128)(2,1)S(1)}, bf16[256,512]{1,0:T(8,128)(2,1)S(1)}, u32[]{:S(2)}, u32[]{:S(2)}) collective-permute-start(bf16[256,512]{1,0:T(8,128)(2,1)S(1)} %fusion.20), channel_id=1, source_target_pairs={{0,16},{1,17},{2,18},{3,19},{4,20},{5,21},{6,22},{7,23},{8,24},{9,... | collective-permute-start | bytes 786440 | tf_op jit(solution)/shard_map/ppermute | solution.py:14
  110.2 3.6 %collective-permute-start.1 = (bf16[256,512]{1,0:T(8,128)(2,1)}, bf16[256,512]{1,0:T(8,128)(2,1)S(1)}, u32[]{:S(2)}, u32[]{:S(2)}) collective-permute-start(bf16[256,512]{1,0:T(8,128)(2,1)} %fusion.21), channel_id=1, source_target_pairs={{0,16},{1,17},{2,18},{3,19},{4,20},{5,21},{6,22},{7,23},{8,24},{9,... | collective-permute-start | bytes 786440 | tf_op jit(solution)/shard_map/ppermute | solution.py:14
  125.3 3.6 %collective-permute-start.2 = (bf16[256,512]{1,0:T(8,128)(2,1)}, bf16[256,512]{1,0:T(8,128)(2,1)S(1)}, u32[]{:S(2)}, u32[]{:S(2)}) collective-permute-start(bf16[256,512]{1,0:T(8,128)(2,1)} %fusion.22), channel_id=1, source_target_pairs={{0,16},{1,17},{2,18},{3,19},{4,20},{5,21},{6,22},{7,23},{8,24},{9,... | collective-permute-start | bytes 786440 | tf_op jit(solution)/shard_map/ppermute | solution.py:14
  139.8 2.7 %copy-start.6 = (bf16[256,512]{1,0:T(8,128)(2,1)}, bf16[256,512]{1,0:T(8,128)(2,1)S(1)}, u32[]{:S(2)}) copy-start(bf16[256,512]{1,0:T(8,128)(2,1)S(1)} %fusion.23) | copy-start | bytes 786436
  139.8 3.4 %collective-permute-start.3 = (bf16[256,512]{1,0:T(8,128)(2,1)S(1)}, bf16[256,512]{1,0:T(8,128)(2,1)S(1)}, u32[]{:S(2)}, u32[]{:S(2)}) collective-permute-start(bf16[256,512]{1,0:T(8,128)(2,1)S(1)} %fusion.23), channel_id=1, source_target_pairs={{0,16},{1,17},{2,18},{3,19},{4,20},{5,21},{6,22},{7,23},{8,24},{9,... | collective-permute-start | bytes 786440 | tf_op jit(solution)/shard_map/ppermute | solution.py:14
  151.6 2.6 %copy-start.7 = (bf16[256,512]{1,0:T(8,128)(2,1)S(1)}, bf16[256,512]{1,0:T(8,128)(2,1)}, u32[]{:S(2)}) copy-start(bf16[256,512]{1,0:T(8,128)(2,1)} %copy-done.6) | copy-start | bytes 786436
  151.6 2.6 %copy-start.14 = (bf16[256,512]{1,0:T(8,128)(2,1)S(1)}, bf16[256,512]{1,0:T(8,128)(2,1)}, u32[]{:S(2)}) copy-start(bf16[256,512]{1,0:T(8,128)(2,1)} %copy-done.13) | copy-start | bytes 786436
  (6 other events, 5.8 us)
where the time goes:
time: 158 us; the launch traced here: 157 us
  local copies, waits for them, and re-layouts  57.7 us (37%)
  matrix products  26.4 us (17%)
  other arithmetic  24.2 us (15%)
  starting transfers between devices  24 us (15%)
  waiting for transfers between devices  23.7 us (15%)
    all_to_all x1, waiting for transfers between devices, regroup_rows(): lax.all_to_all(outgoing, 'seq', split_axis=0, concat_axis=0, tiled=True)  16 us
    dot_general x5, matrix products, hstu_block(): jnp.einsum('hij,jhd->ihd', attend_weights, value_part, preferred_element_...  13.5 us
    unnamed x53, local copies, waits for them, and re-layouts  9.74 us
    ppermute x4, starting transfers between devices, shifted(): return lax.ppermute(shard, axis, pairs)  8.39 us
    dot_general x5, matrix products, hstu_block(): jnp.dot(gated, w_out, preferred_element_type=jnp.float32)  8.21 us
    all_to_all x1, starting transfers between devices, fetch_rows(): lax.all_to_all(asked_rows, 'table', split_axis=0, concat_axis=0, tiled=True)  7.28 us
    another operation x2, local copies, waits for them, and re-layouts, bias_grid(): tiled = jnp.tile(flipped, (1, row_count + 1))  6.85 us
    reshape x5, local copies, waits for them, and re-layouts, hstu_block(): attended = attended.reshape(row_count, model_width)  5.93 us
  transfers between devices with their start and end apart: 7, of which 6 were waited for; matrix products, arithmetic and copies ran while one was open for 18% of the time, Pallas kernels for 0%

commit v1 on v0

--- a/solution.py
+++ b/solution.py
@@ -14,6 +14,11 @@
     return lax.ppermute(shard, axis, pairs)
 
 
+def running_sum(counts):
+    places = jnp.arange(counts.shape[0])
+    return jnp.sum(jnp.where(places[None, :] <= places[:, None], counts[None, :], 0), axis=1)
+
+
 def layer_norm(values, gain_row):
     center = values - jnp.mean(values, axis=-1, keepdims=True)
     spread = jnp.mean(center * center, axis=-1, keepdims=True)
@@ -21,7 +26,7 @@
 
 
 def user_mask(lengths, row_count):
-    limits = jnp.cumsum(lengths)
+    limits = running_sum(lengths)
     places = jnp.arange(row_count, dtype=jnp.int32)
     owners = jnp.sum((places[:, None] >= limits[None, :]).astype(jnp.int32), axis=1)
     return (owners[:, None] == owners[None, :]) & (places[None, :] <= places[:, None])
@@ -72,7 +77,7 @@
 def fetch_rows(slab_part, request_rows, owner_counts, item_slots):
     row_counts = owner_counts[0]
     owner_total = row_counts.shape[0]
-    limits = jnp.cumsum(row_counts)
+    limits = running_sum(row_counts)
     firsts = limits - row_counts
     offsets = jnp.arange(CAP, dtype=jnp.int32)
     listed = request_rows[0]
@@ -96,14 +101,14 @@
     capacity = token_count // peer_count + token_count // (2 * peer_count)
     seq_index = lax.axis_index("seq")
     sent_counts = send_plan[seq_index]
-    send_start = jnp.cumsum(sent_counts) - sent_counts
+    send_start = running_sum(sent_counts) - sent_counts
     take_index = jnp.minimum(
         send_start[:, None] + jnp.arange(capacity, dtype=jnp.int32)[None, :], token_count - 1
     )
     outgoing = event_rows[take_index]
     incoming = lax.all_to_all(outgoing, "seq", split_axis=0, concat_axis=0, tiled=True)
     got_counts = send_plan[:, seq_index]
-    recv_last = jnp.cumsum(got_counts)
+    recv_last = running_sum(got_counts)
     recv_first = recv_last - got_counts
     places = jnp.arange(token_count, dtype=jnp.int32)
     sources = jnp.sum((places[:, None] >= recv_last[None, :]).astype(jnp.int32), axis=1)

time: 158 us -> 155 us (0.981)
  other arithmetic: 24.2 us -> 22.4 us
    another operation x9 -> x0, other arithmetic: 2.26 us -> none
    unnamed x53 -> x61, local copies, waits for them, and re-layouts: 9.74 us -> 9.76 us
  transfers between devices with their start and end apart: 7 -> 7, of which waited for: 6 -> 6; matrix products, arithmetic and copies ran while one was open for 18% -> 17% of each run, Pallas kernels for 0% -> 0%
where the time goes in v1:
time: 155 us; the launch traced here: 154 us
  local copies, waits for them, and re-layouts  57.7 us (37%)
  matrix products  25 us (16%)
  starting transfers between devices  24 us (15%)
  waiting for transfers between devices  23.7 us (15%)
  other arithmetic  22.4 us (14%)
    all_to_all x1, waiting for transfers between devices, regroup_rows(): lax.all_to_all(outgoing, 'seq', split_axis=0, concat_axis=0, tiled=True)  16 us
    dot_general x5, matrix products, hstu_block(): jnp.einsum('hij,jhd->ihd', attend_weights, value_part, preferred_element_...  13.5 us
    unnamed x61, local copies, waits for them, and re-layouts  9.76 us
    ppermute x4, starting transfers between devices, shifted(): return lax.ppermute(shard, axis, pairs)  8.43 us
    all_to_all x1, starting transfers between devices, fetch_rows(): lax.all_to_all(asked_rows, 'table', split_axis=0, concat_axis=0, tiled=True)  7.28 us
    another operation x2, local copies, waits for them, and re-layouts, bias_grid(): tiled = jnp.tile(flipped, (1, row_count + 1))  6.85 us
    dot_general x5, matrix products, hstu_block(): jnp.dot(gated, w_out, preferred_element_type=jnp.float32)  6.81 us
    reshape x5, local copies, waits for them, and re-layouts, hstu_block(): attended = attended.reshape(row_count, model_width)  5.93 us
  transfers between devices with their start and end apart: 7, of which 6 were waited for; matrix products, arithmetic and copies ran while one was open for 17% of the time, Pallas kernels for 0%

profile of v1, /device:TPU:0, one launch (start us, length us, event | category | flops | bytes accessed | tf_op | source)
XLA Modules:
  0.0 153.5 jit_solution(4399842515119436512)
XLA Ops:
  1.8 3.5 %gather_fusion = s32[512]{0:T(512)S(1)} fusion(s32[512]{0:T(512)S(1)} %bitcast.225, s32[1024]{0:T(1024)S(1)} %pad_clamp_fusion.2), kind=kCustom, calls=%fused_computation | custom fusion | bytes 6144 | tf_op jit(solution)/shard_map/gather | solution.py:86
  6.1 7.3 %all-to-all-start = ((s32[8,1,64]{2,1,0:T(1,128)}), s32[8,1,64]{2,1,0:T(1,128)S(1)}, u32[]{:S(2)}, u32[]{:S(2)}) async-start(s32[8,1,64]{2,1,0:T(1,128)} %compare_select_fusion.12), calls=%async_computation | async-start | bytes 8192 | tf_op jit(solution)/shard_map/all_to_all | solution.py:88
  15.5 4.3 %all-to-all-done = s32[8,1,64]{2,1,0:T(1,128)S(1)} async-done(((s32[8,1,64]{2,1,0:T(1,128)}), s32[8,1,64]{2,1,0:T(1,128)S(1)}, u32[]{:S(2)}, u32[]{:S(2)}) %all-to-all-start) | async-done | bytes 2080 | tf_op jit(solution)/shard_map/all_to_all | solution.py:88
  19.9 2.6 %gather_fusion.1 = bf16[512,512]{1,0:T(8,128)(2,1)} fusion(bf16[1024,512]{1,0:T(8,128)(2,1)S(1)} %copy-done.3, s32[1024]{0:T(1024)S(1)} %pad_clamp_fusion.1), kind=kCustom, calls=%fused_computation.1 | custom fusion | bytes 1050624 | tf_op jit(solution)/shard_map/gather | solution.py:87
  22.5 3.5 %all-to-all-start.1 = ((bf16[8,64,512]{2,1,0:T(8,128)(2,1)}), bf16[8,64,512]{2,1,0:T(8,128)(2,1)S(1)}, u32[]{:S(2)}, u32[]{:S(2)}) async-start(bf16[8,64,512]{2,1,0:T(8,128)(2,1)} %bitcast.233), calls=%async_computation.1 | async-start | bytes 1048576 | tf_op jit(solution)/shard_map/all_to_all | solution.py:90
  26.6 1.6 %tile.4 = f32[4,257,511]{2,1,0:T(8,128)} broadcast(f32[4,511]{1,0:T(4,128)S(1)} %slice.258), dimensions={0,2} | broadcast | bytes 2109408 | tf_op jit(solution)/shard_map/tile | solution.py:41
  28.3 5.2 %tile.10 = f32[4,131327]{1,0:T(4,128)} reshape(f32[4,257,511]{2,1,0:T(8,128)} %tile.4) | data formatting | bytes 4202464 | tf_op jit(solution)/shard_map/tile | solution.py:41
  33.5 4.1 %slice.165 = f32[4,130560]{1,0:T(4,128)} slice(f32[4,131327]{1,0:T(4,128)} %tile.10), slice={[0:4], [255:130815]} | slice | bytes 4177920 | tf_op jit(solution)/shard_map/slice | solution.py:43
  37.5 5.4 %reshape.735 = f32[4,256,510]{2,1,0:T(8,128)} reshape(f32[4,130560]{1,0:T(4,128)} %slice.165) | data formatting | bytes 4177920 | tf_op jit(solution)/shard_map/reshape | solution.py:44
  43.0 4.3 %compare_select_fusion.6 = s32[1024,1]{0,1:T(1,128)S(1)} fusion(s32[]{:T(128)} %bitcast.9, s32[]{:T(128)} %bitcast.10, s32[]{:T(128)} %bitcast.11, s32[]{:T(128)} %bitcast.12, s32[]{:T(128)} %bitcast.13, s32[]{:T(128)} %bitcast.15, s32[]{:T(128)} %bitcast.14, s32[1024,1]{0,1:T(1,128)S(1)} %bitcast.244), kind=kLoop, calls=%fused_computation.221 | loop fusion | flops 15360 | bytes 8220 | tf_op jit(solution)/shard_map/gather | solution.py:93
  48.8 5.1 %gather_fusion.2 = bf16[1024,512]{1,0:T(8,128)(2,1)S(1)} fusion(bf16[512,512]{1,0:T(8,128)(2,1)} %bitcast.226, s32[1024]{0:T(1024)S(1)} %broadcast_clamp_fusion.1), kind=kCustom, calls=%fused_computation.2 | custom fusion | bytes 2101248 | tf_op jit(solution)/shard_map/gather | solution.py:94
  53.9 5.4 %gather_fusion.3 = bf16[1536,512]{1,0:T(8,128)(2,1)} fusion(bf16[1024,512]{1,0:T(8,128)(2,1)S(1)} %gather_fusion.2, s32[2048]{0:T(1024)S(1)} %pad_clamp_fusion), kind=kCustom, calls=%fused_computation.3 | custom fusion | bytes 3151872 | tf_op jit(solution)/shard_map/gather | solution.py:108
  59.4 4.8 %all-to-all-start.2 = ((bf16[2,768,512]{2,1,0:T(8,128)(2,1)}), bf16[2,768,512]{2,1,0:T(8,128)(2,1)}, u32[]{:S(2)}, u32[]{:S(2)}) async-start(bf16[2,768,512]{2,1,0:T(8,128)(2,1)} %bitcast.227), calls=%async_computation.2 | async-start | bytes 3145728 | tf_op jit(solution)/shard_map/all_to_all | solution.py:109
  66.2 16.0 %all-to-all-done.2 = bf16[2,768,512]{2,1,0:T(8,128)(2,1)} async-done(((bf16[2,768,512]{2,1,0:T(8,128)(2,1)}), bf16[2,768,512]{2,1,0:T(8,128)(2,1)}, u32[]{:S(2)}, u32[]{:S(2)}) %all-to-all-start.2) | async-done | bytes 1572896 | tf_op jit(solution)/shard_map/all_to_all | solution.py:109
  82.2 5.6 %gather_fusion.4 = bf16[1024,512]{1,0:T(8,128)(2,1)S(1)} fusion(bf16[1536,512]{1,0:T(8,128)(2,1)} %bitcast.21, s32[1024]{0:T(1024)S(1)} %broadcast_clamp_fusion), kind=kCustom, calls=%fused_computation.4 | custom fusion | bytes 2101248 | tf_op jit(solution)/shard_map/gather | solution.py:116
  91.1 2.2 %fusion.205 = (f32[256]{0:T(256)S(1)}, f32[4,128,256]{2,1,0:T(8,128)S(1)}) fusion(bf16[256,4,128]{0,2,1:T(8,128)(2,1)} %bitcast.239, f32[4,256,510]{2,1,0:T(8,128)} %reshape.735, pred[256,256]{1,0:T(8,128)(4,1)S(1)} %fusion.173, bf16[32,4,8,128]{3,2,1,0:T(8,128)(2,1)} %get-tuple-element.28, bf16[32,4,8,128]{3,2,1,0:T(8,128)(2,1)} %get-tuple-element.27), kind=kOutput, calls=%fused_computation.312 | convolution fusion | flops 136445696 | bytes 2425856 | tf_op jit(solution)/shard_map/hij,jhd->ihd/dot_general | solution.py:67
  94.5 1.5 %fusion.20 = bf16[256,512]{1,0:T(8,128)(2,1)S(1)} fusion(bf16[1,512,512]{2,1,0:T(8,128)(2,1)S(1)} %copy-done.4, f32[256,512]{1,0:T(8,128)} %copy.74, bf16[256,2048]{1,0:T(8,128)(2,1)} %copy-done.16, f32[512]{0:T(512)S(1)} %bitcast.246, f32[256]{0:T(256)S(1)} %add_rsqrt_fusion.8, f32[256]{0:T(256)S(1)} %broadcast_multiply_fusion.8, ...), kind=kOutput, calls=%fused_computation.35 | convolution fusion | flops 135397376 | bytes 1839104 | tf_op jit(solution)/shard_map/dot_general | solution.py:72
  102.7 2.8 %fusion.210 = (f32[256]{0:T(256)S(1)}, f32[4,128,256]{2,1,0:T(8,128)}) fusion(bf16[256,4,128]{0,2,1:T(8,128)(2,1)S(1)} %bitcast.240, f32[4,256,510]{2,1,0:T(8,128)} %reshape.735, pred[256,256]{1,0:T(8,128)(4,1)S(1)} %fusion.172, bf16[32,4,8,128]{3,2,1,0:T(8,128)(2,1)} %get-tuple-element.25, bf16[32,4,8,128]{3,2,1,0:T(8,128)(2,1)} %get-tuple-element.24), kind=kOutput, calls=%fused_computation.313 | convolution fusion | flops 136445696 | bytes 2425856 | tf_op jit(solution)/shard_map/hij,jhd->ihd/dot_general | solution.py:67
  109.3 2.3 %collective-permute-start.1 = (bf16[256,512]{1,0:T(8,128)(2,1)S(1)}, bf16[256,512]{1,0:T(8,128)(2,1)S(1)}, u32[]{:S(2)}, u32[]{:S(2)}) collective-permute-start(bf16[256,512]{1,0:T(8,128)(2,1)S(1)} %fusion.21), channel_id=1, source_target_pairs={{0,16},{1,17},{2,18},{3,19},{4,20},{5,21},{6,22},{7,23},{8,24},{9,... | collective-permute-start | bytes 786440 | tf_op jit(solution)/shard_map/ppermute | solution.py:14
  117.0 2.8 %fusion.215 = (f32[256]{0:T(256)S(1)}, f32[4,128,256]{2,1,0:T(8,128)}) fusion(bf16[256,4,128]{0,2,1:T(8,128)(2,1)S(1)} %bitcast.241, f32[4,256,510]{2,1,0:T(8,128)} %reshape.735, pred[256,256]{1,0:T(8,128)(4,1)S(1)} %fusion.171, bf16[32,4,8,128]{3,2,1,0:T(8,128)(2,1)} %get-tuple-element.22, bf16[32,4,8,128]{3,2,1,0:T(8,128)(2,1)} %get-tuple-element.21), kind=kOutput, calls=%fused_computation.314 | convolution fusion | flops 136445696 | bytes 2425856 | tf_op jit(solution)/shard_map/hij,jhd->ihd/dot_general | solution.py:67
  123.6 2.3 %collective-permute-start.2 = (bf16[256,512]{1,0:T(8,128)(2,1)S(1)}, bf16[256,512]{1,0:T(8,128)(2,1)S(1)}, u32[]{:S(2)}, u32[]{:S(2)}) collective-permute-start(bf16[256,512]{1,0:T(8,128)(2,1)S(1)} %fusion.22), channel_id=1, source_target_pairs={{0,16},{1,17},{2,18},{3,19},{4,20},{5,21},{6,22},{7,23},{8,24},{9,... | collective-permute-start | bytes 786440 | tf_op jit(solution)/shard_map/ppermute | solution.py:14
  131.3 2.8 %fusion.220 = (f32[256]{0:T(256)S(1)}, f32[4,128,256]{2,1,0:T(8,128)}) fusion(bf16[256,4,128]{0,2,1:T(8,128)(2,1)S(1)} %bitcast.242, f32[4,256,510]{2,1,0:T(8,128)} %reshape.735, pred[256,256]{1,0:T(8,128)(4,1)S(1)} %fusion.170, bf16[32,4,8,128]{3,2,1,0:T(8,128)(2,1)} %get-tuple-element.19, bf16[32,4,8,128]{3,2,1,0:T(8,128)(2,1)} %get-tuple-element.18), kind=kOutput, calls=%fused_computation.315 | convolution fusion | flops 136445696 | bytes 2425856 | tf_op jit(solution)/shard_map/hij,jhd->ihd/dot_general | solution.py:67
  137.8 2.5 %collective-permute-start.3 = (bf16[256,512]{1,0:T(8,128)(2,1)S(1)}, bf16[256,512]{1,0:T(8,128)(2,1)S(1)}, u32[]{:S(2)}, u32[]{:S(2)}) collective-permute-start(bf16[256,512]{1,0:T(8,128)(2,1)S(1)} %fusion.23), channel_id=1, source_target_pairs={{0,16},{1,17},{2,18},{3,19},{4,20},{5,21},{6,22},{7,23},{8,24},{9,... | collective-permute-start | bytes 786440 | tf_op jit(solution)/shard_map/ppermute | solution.py:14
  145.6 2.8 %fusion.225 = (f32[256]{0:T(256)S(1)}, f32[4,128,256]{2,1,0:T(8,128)}) fusion(bf16[256,4,128]{0,2,1:T(8,128)(2,1)S(1)} %bitcast.238, f32[4,256,510]{2,1,0:T(8,128)} %reshape.735, pred[256,256]{1,0:T(8,128)(4,1)S(1)} %fusion.169, bf16[32,4,8,128]{3,2,1,0:T(8,128)(2,1)} %get-tuple-element.16, bf16[32,4,8,128]{3,2,1,0:T(8,128)(2,1)} %get-tuple-element.15), kind=kOutput, calls=%fused_computation.316 | convolution fusion | flops 136445696 | bytes 2425856 | tf_op jit(solution)/shard_map/hij,jhd->ihd/dot_general | solution.py:67
  (169 shorter events, 51.8 us)
Async XLA Ops:
  0.0 88.2 %copy-start = (bf16[1,512,2048]{2,1,0:T(8,128)(2,1)S(1)}, bf16[1,512,2048]{2,1,0:T(8,128)(2,1)}, u32[]{:S(2)}) copy-start(bf16[1,512,2048]{2,1,0:T(8,128)(2,1)} %param.18) | copy-start | bytes 6291460
  1.8 3.7 %copy-start.24 = (s32[1,8]{1,0:T(1,128)S(1)}, s32[1,8]{1,0:T(1,128)}, u32[]{:S(2)}) copy-start(s32[1,8]{1,0:T(1,128)} %param.14) | copy-start | bytes 100
  1.8 12.3 %copy-start.22 = (s32[1,2,2]{2,1,0:T(2,128)S(1)}, s32[1,2,2]{2,1,0:T(2,128)}, u32[]{:S(2)}) copy-start(s32[1,2,2]{2,1,0:T(2,128)} %param.16) | copy-start | bytes 52
  1.8 12.5 %copy-start.21 = (s32[1,1024]{1,0:T(1,128)S(1)}, s32[1,1024]{1,0:T(1,128)}, u32[]{:S(2)}) copy-start(s32[1,1024]{1,0:T(1,128)} %param.15) | copy-start | bytes 12292
  1.8 13.0 %copy-start.23 = (s32[4,8]{1,0:T(4,128)S(1)}, s32[4,8]{1,0:T(4,128)}, u32[]{:S(2)}) copy-start(s32[4,8]{1,0:T(4,128)} %param.17) | copy-start | bytes 388
  1.8 13.5 %copy-start.20 = (f32[1,4,128]{2,1,0:T(4,128)S(1)}, f32[1,4,128]{2,1,0:T(4,128)}, u32[]{:S(2)}) copy-start(f32[1,4,128]{2,1,0:T(4,128)} %param.22) | copy-start | bytes 6148
  1.8 18.0 %copy-start.3 = (bf16[1024,512]{1,0:T(8,128)(2,1)S(1)}, bf16[1024,512]{1,0:T(8,128)(2,1)}, u32[]{:S(2)}) copy-start(bf16[1024,512]{1,0:T(8,128)(2,1)} %param.12) | copy-start | bytes 3145732
  6.1 13.7 %all-to-all-start = ((s32[8,1,64]{2,1,0:T(1,128)}), s32[8,1,64]{2,1,0:T(1,128)S(1)}, u32[]{:S(2)}, u32[]{:S(2)}) async-start(s32[8,1,64]{2,1,0:T(1,128)} %compare_select_fusion.12), calls=%async_computation | async-start | bytes 8192 | tf_op jit(solution)/shard_map/all_to_all | solution.py:88
  22.5 25.6 %all-to-all-start.1 = ((bf16[8,64,512]{2,1,0:T(8,128)(2,1)}), bf16[8,64,512]{2,1,0:T(8,128)(2,1)S(1)}, u32[]{:S(2)}, u32[]{:S(2)}) async-start(bf16[8,64,512]{2,1,0:T(8,128)(2,1)} %bitcast.233), calls=%async_computation.1 | async-start | bytes 1048576 | tf_op jit(solution)/shard_map/all_to_all | solution.py:90
  59.4 22.8 %all-to-all-start.2 = ((bf16[2,768,512]{2,1,0:T(8,128)(2,1)}), bf16[2,768,512]{2,1,0:T(8,128)(2,1)}, u32[]{:S(2)}, u32[]{:S(2)}) async-start(bf16[2,768,512]{2,1,0:T(8,128)(2,1)} %bitcast.227), calls=%async_computation.2 | async-start | bytes 3145728 | tf_op jit(solution)/shard_map/all_to_all | solution.py:109
  82.2 6.0 %copy-start.25 = (f32[1,2048]{1,0:T(1,128)S(1)}, f32[1,2048]{1,0:T(1,128)}, u32[]{:S(2)}) copy-start(f32[1,2048]{1,0:T(1,128)} %param.19) | copy-start | bytes 24580
  82.2 6.0 %copy-start.26 = (f32[1,512]{1,0:T(1,128)S(1)}, f32[1,512]{1,0:T(1,128)}, u32[]{:S(2)}) copy-start(f32[1,512]{1,0:T(1,128)} %param.20) | copy-start | bytes 6148
  91.1 3.3 %copy-start.4 = (bf16[1,512,512]{2,1,0:T(8,128)(2,1)S(1)}, bf16[1,512,512]{2,1,0:T(8,128)(2,1)}, u32[]{:S(2)}) copy-start(bf16[1,512,512]{2,1,0:T(8,128)(2,1)} %param.23) | copy-start | bytes 1572868
  91.1 3.3 %copy-start.19 = (f32[1,512]{1,0:T(1,128)S(1)}, f32[1,512]{1,0:T(1,128)}, u32[]{:S(2)}) copy-start(f32[1,512]{1,0:T(1,128)} %param.21) | copy-start | bytes 6148
  96.0 3.8 %copy-start.17 = (bf16[256,512]{1,0:T(8,128)(2,1)}, bf16[256,512]{1,0:T(8,128)(2,1)S(1)}, u32[]{:S(2)}) copy-start(bf16[256,512]{1,0:T(8,128)(2,1)S(1)} %fusion.20) | copy-start | bytes 786436
  96.0 2.4 %collective-permute-start = (bf16[256,512]{1,0:T(8,128)(2,1)S(1)}, bf16[256,512]{1,0:T(8,128)(2,1)S(1)}, u32[]{:S(2)}, u32[]{:S(2)}) collective-permute-start(bf16[256,512]{1,0:T(8,128)(2,1)S(1)} %fusion.20), channel_id=1, source_target_pairs={{0,16},{1,17},{2,18},{3,19},{4,20},{5,21},{6,22},{7,23},{8,24},{9,... | collective-permute-start | bytes 786440 | tf_op jit(solution)/shard_map/ppermute | solution.py:14
  109.3 3.4 %collective-permute-start.1 = (bf16[256,512]{1,0:T(8,128)(2,1)S(1)}, bf16[256,512]{1,0:T(8,128)(2,1)S(1)}, u32[]{:S(2)}, u32[]{:S(2)}) collective-permute-start(bf16[256,512]{1,0:T(8,128)(2,1)S(1)} %fusion.21), channel_id=1, source_target_pairs={{0,16},{1,17},{2,18},{3,19},{4,20},{5,21},{6,22},{7,23},{8,24},{9,... | collective-permute-start | bytes 786440 | tf_op jit(solution)/shard_map/ppermute | solution.py:14
  123.6 3.4 %collective-permute-start.2 = (bf16[256,512]{1,0:T(8,128)(2,1)S(1)}, bf16[256,512]{1,0:T(8,128)(2,1)S(1)}, u32[]{:S(2)}, u32[]{:S(2)}) collective-permute-start(bf16[256,512]{1,0:T(8,128)(2,1)S(1)} %fusion.22), channel_id=1, source_target_pairs={{0,16},{1,17},{2,18},{3,19},{4,20},{5,21},{6,22},{7,23},{8,24},{9,... | collective-permute-start | bytes 786440 | tf_op jit(solution)/shard_map/ppermute | solution.py:14
  137.8 2.7 %copy-start.10 = (bf16[256,512]{1,0:T(8,128)(2,1)}, bf16[256,512]{1,0:T(8,128)(2,1)S(1)}, u32[]{:S(2)}) copy-start(bf16[256,512]{1,0:T(8,128)(2,1)S(1)} %fusion.23) | copy-start | bytes 786436
  137.8 3.4 %collective-permute-start.3 = (bf16[256,512]{1,0:T(8,128)(2,1)S(1)}, bf16[256,512]{1,0:T(8,128)(2,1)S(1)}, u32[]{:S(2)}, u32[]{:S(2)}) collective-permute-start(bf16[256,512]{1,0:T(8,128)(2,1)S(1)} %fusion.23), channel_id=1, source_target_pairs={{0,16},{1,17},{2,18},{3,19},{4,20},{5,21},{6,22},{7,23},{8,24},{9,... | collective-permute-start | bytes 786440 | tf_op jit(solution)/shard_map/ppermute | solution.py:14
  149.7 2.6 %copy-start.7 = (bf16[256,512]{1,0:T(8,128)(2,1)S(1)}, bf16[256,512]{1,0:T(8,128)(2,1)}, u32[]{:S(2)}) copy-start(bf16[256,512]{1,0:T(8,128)(2,1)} %copy-done.6) | copy-start | bytes 786436
  149.7 2.6 %copy-start.9 = (bf16[256,512]{1,0:T(8,128)(2,1)S(1)}, bf16[256,512]{1,0:T(8,128)(2,1)}, u32[]{:S(2)}) copy-start(bf16[256,512]{1,0:T(8,128)(2,1)} %copy-done.8) | copy-start | bytes 786436
  149.7 2.6 %copy-start.11 = (bf16[256,512]{1,0:T(8,128)(2,1)S(1)}, bf16[256,512]{1,0:T(8,128)(2,1)}, u32[]{:S(2)}) copy-start(bf16[256,512]{1,0:T(8,128)(2,1)} %copy-done.10) | copy-start | bytes 786436
  149.7 2.6 %copy-start.18 = (bf16[256,512]{1,0:T(8,128)(2,1)S(1)}, bf16[256,512]{1,0:T(8,128)(2,1)}, u32[]{:S(2)}) copy-start(bf16[256,512]{1,0:T(8,128)(2,1)} %copy-done.17) | copy-start | bytes 786436
  (10 other events, 14.0 us)

commit v2 on v0

v2 whole, which is shorter than its diff:
```python
import functools

import jax
import jax.numpy as jnp
from jax import lax
from jax.experimental import pallas as pl
from jax.experimental.pallas import tpu as pltpu
from jax.sharding import PartitionSpec as P

HEADS = 4
MB_TOK = 256
CAP = 64
LANES = 128
MESH = pl.DeviceIdType.MESH
F32 = jnp.float32
BF16 = jnp.bfloat16


def iota(shape, axis):
    return lax.broadcasted_iota(jnp.int32, shape, axis)


def normalise(values):
    center = values - jnp.mean(values, axis=-1, keepdims=True)
    spread = jnp.mean(center * center, axis=-1, keepdims=True)
    return center * lax.rsqrt(spread + 1e-05)


def silu_of_half(half):
    return half + half * jnp.tanh(half)


def kernel(
    dims,
    slab_hbm,
    req_ref,
    counts_smem,
    slots_ref,
    plan_smem,
    lengths_smem,
    wp_hbm,
    bias_ref,
    gin_ref,
    gmid_ref,
    rel_ref,
    wo_hbm,
    out_ref,
    slab,
    wp,
    wo,
    par,
    msg,
    flat,
    ids,
    gath,
    rows,
    grid,
    mask,
    made,
    local_sem,
    wsend,
    wrecv,
    msend,
    mrecv,
    fsend,
    frecv,
    rsend,
    rrecv,
    xsend,
    xrecv,
    ssend,
    srecv,
    osend,
    orecv,
):
    peers, tables = dims
    half = CAP // 2
    width = slab.shape[1]
    span = LANES
    tokens = slots_ref.shape[1]
    mine = tokens // 2
    micro = mine // MB_TOK
    listed = req_ref.shape[1] // LANES
    slab_rows = slab.shape[0]
    block_rows = 2 * tables * half
    users = lengths_smem.shape[1]
    head_size = width // HEADS
    c = lax.axis_index("section")
    s = lax.axis_index("seq")
    t = lax.axis_index("table")
    sib = (1 - c, s, t)

    def table_peer(k):
        return lax.rem(t + k, tables)

    def seq_peer(k):
        return lax.rem(s + k, peers)

    def remote(src, dst, send, recv, to):
        return pltpu.make_async_remote_copy(
            src_ref=src,
            dst_ref=dst,
            send_sem=send,
            recv_sem=recv,
            device_id=to,
            device_id_type=MESH,
        )

    slab_copy = pltpu.make_async_copy(slab_hbm, slab, local_sem.at[0])
    wp_copy = pltpu.make_async_copy(wp_hbm.at[0], wp.at[c], local_sem.at[1])
    wo_copy = pltpu.make_async_copy(wo_hbm.at[0], wo.at[c], local_sem.at[2])
    slab_copy.start()
    wp_copy.start()
    wo_copy.start()

    barrier = pltpu.get_barrier_semaphore()

    def greet_table(k, carry):
        pl.semaphore_signal(barrier, inc=1, device_id=(c, s, table_peer(k)), device_id_type=MESH)
        return carry

    def greet_seq(k, carry):
        pl.semaphore_signal(barrier, inc=1, device_id=(c, seq_peer(k), t), device_id_type=MESH)
        return carry

    lax.fori_loop(1, tables, greet_table, 0)
    lax.fori_loop(1, peers, greet_seq, 0)
    pl.semaphore_signal(barrier, inc=1, device_id=sib, device_id_type=MESH)

    for k in range(listed):
        msg[t, k : k + 1, :] = req_ref[0:1, k * LANES : (k + 1) * LANES]
    lane = iota((1, LANES), 1)
    first_row = jnp.zeros((1, LANES), jnp.int32)
    limit = jnp.int32(0)
    limits = []
    for o in range(tables):
        first_row = jnp.where(lane == o, limit, first_row)
        limit = limit + counts_smem[0, o]
        limits.append(limit)
    msg[t, listed : listed + 1, :] = first_row

    for k in range(tokens // LANES):
        slot = slots_ref[0:1, k * LANES : (k + 1) * LANES]
        owner = jnp.zeros((1, LANES), jnp.int32)
        first = jnp.zeros((1, LANES), jnp.int32)
        for o in range(tables):
            past = slot >= limits[o]
            owner = owner + jnp.where(past, 1, 0)
            first = jnp.where(past, limits[o], first)
        place = slot - first
        place = place + owner * half + jnp.where(place >= half, (tables - 1) * half, 0)
        flat[s, k : k + 1, :] = place

    for k in range(4):
        par[c, k : k + 1, :] = bias_ref[0:1, k * width : (k + 1) * width] * 0.5
    par[c, 4:5, :] = gin_ref[...]
    par[c, 5:6, :] = gmid_ref[...]
    for k in range(HEADS):
        par[c, 8 + k : 9 + k, 0:span] = rel_ref[0, k : k + 1, :] * 0.5

    pl.semaphore_wait(barrier, (tables - 1) + (peers - 1) + 1)

    def ask(k):
        return remote(msg.at[t], msg.at[t], msend.at[k], mrecv.at[t], (c, s, table_peer(k)))

    def ask_step(k, carry):
        ask(k).start()
        return carry

    lax.fori_loop(1, tables, ask_step, 0)

    def tell(k):
        return remote(flat.at[s], flat.at[s], fsend.at[k], frecv.at[s], (c, seq_peer(k), t))

    def tell_step(k, carry):
        tell(k).start()
        return carry

    lax.fori_loop(1, peers, tell_step, 0)
    par_copy = remote(par.at[c], par.at[c], wsend.at[0], wrecv.at[0], sib)
    wp_send = remote(wp_hbm.at[0], wp.at[c], wsend.at[1], wrecv.at[1], sib)
    wo_send = remote(wo_hbm.at[0], wo.at[c], wsend.at[2], wrecv.at[2], sib)
    par_copy.start()
    wp_send.start()
    wo_send.start()

    lower = MB_TOK // 2
    for m in range(micro):
        row_owner = jnp.zeros((1, MB_TOK), jnp.int32)
        col_owner = jnp.zeros((MB_TOK, 1), jnp.int32)
        place_row = iota((1, MB_TOK), 1)
        place_col = iota((MB_TOK, 1), 0)
        end = jnp.int32(0)
        for u in range(users):
            end = end + lengths_smem[c * micro + m, u]
            row_owner = row_owner + jnp.where(place_row >= end, 1, 0)
            col_owner = col_owner + jnp.where(place_col >= end, 1, 0)
        top = (col_owner[:lower] == row_owner[:, :lower]) & (place_row[:, :lower] <= place_col[:lower])
        low = (col_owner[lower:] == row_owner) & (place_row <= place_col[lower:])
        mask[m, :, 0:lower] = jnp.where(top, 1.0, 0.0)
        mask[m, :, lower:] = jnp.where(low, 1.0, 0.0)

    def hear(k, carry):
        o = table_peer(k)
        remote(msg.at[o], msg.at[o], msend.at[k], mrecv.at[o], (c, s, o)).wait_recv()
        return carry

    lax.fori_loop(1, tables, hear, 0)

    def read_ids(o, carry):
        firsts = msg[o, listed : listed + 1, :]
        first = jnp.sum(jnp.where(lane == t, firsts, 0).astype(F32), axis=1, keepdims=True)
        want = first.astype(jnp.int32) + c * half + iota((half, LANES), 0)
        total = jnp.zeros((half, LANES), F32)
        for k in range(listed):
            listed_row = msg[o, k : k + 1, :].astype(F32)
            total = total + jnp.where(iota((half, LANES), 1) + k * LANES == want, listed_row, 0.0)
        found = jnp.sum(total, axis=1, keepdims=True).astype(jnp.int32)
        ids[o] = jnp.broadcast_to(found, (half, LANES))
        return carry

    lax.fori_loop(0, tables, read_ids, 0)
    slab_copy.wait()
    wanted = ids[...].reshape(tables * half, LANES)
    spots = iota((tables * half, LANES), 1)
    picks = jnp.concatenate(
        [jnp.where(wanted == spots + k * LANES, 1.0, 0.0).astype(BF16) for k in range(slab_rows // LANES)],
        axis=1,
    )
    looked_up = jnp.dot(picks, slab[...], preferred_element_type=F32).astype(BF16)
    gath[...] = looked_up.reshape(tables, half, width)

    def serve(k):
        o = table_peer(k)
        return remote(gath.at[o], rows.at[s, c, t], rsend.at[k], rrecv.at[t], (c, s, o))

    def serve_step(k, carry):
        serve(k).start()
        return carry

    lax.fori_loop(1, tables, serve_step, 0)
    rows[s, c, t] = gath[t]

    def across(k, o):
        place = rows.at[s, c, o]
        return remote(place, place, xsend.at[k, o], xrecv.at[s, o], (c, seq_peer(k), t))

    def beside(source, o):
        place = rows.at[source, c, o]
        return remote(place, place, ssend.at[source, o], srecv.at[source, o], sib)

    def pass_on(o):
        def one(k, carry):
            across(k, o).start()
            return carry

        lax.fori_loop(1, peers, one, 0)
        beside(s, o).start()

    pass_on(t)

    wp_copy.wait()
    wo_copy.wait()
    par_copy.wait_recv()
    for layer in range(2):
        for head in range(HEADS):
            rel_row = jnp.broadcast_to(par[layer, 8 + head : 9 + head, 0:span], (span, span))
            rel_col = jnp.sum(
                jnp.where(iota((span, span), 0) == iota((span, span), 1), rel_row, 0.0), axis=1, keepdims=True
            )
            turned = jnp.where(
                iota((span, 2 * span), 0) + iota((span, 2 * span), 1) == span, rel_col, 0.0
            )
            base = jnp.broadcast_to(jnp.sum(turned, axis=0, keepdims=True), (span, 2 * span))
            grid[layer, head] = pltpu.roll(base, 0, 1, stride=1, stride_axis=0)

    def heard(k, carry):
        source = seq_peer(k)
        remote(flat.at[source], flat.at[source], fsend.at[k], frecv.at[source], (c, source, t)).wait_recv()
        return carry

    lax.fori_loop(1, peers, heard, 0)

    def collect(k, carry):
        o = table_peer(k)
        remote(gath.at[o], rows.at[s, c, o], rsend.at[k], rrecv.at[o], (c, s, o)).wait_recv()
        pass_on(o)
        return carry

    lax.fori_loop(1, tables, collect, 0)

    def second(i, carry):
        source = seq_peer(1 + i // tables)
        o = table_peer(lax.rem(i, tables))
        place = rows.at[source, c, o]
        remote(place, place, xsend.at[1, o], xrecv.at[source, o], (c, source, t)).wait_recv()
        beside(source, o).start()
        return carry

    chunk = mine
    places = iota((chunk, LANES), 0) + c * mine
    total = jnp.zeros((chunk, LANES), F32)
    for source in range(peers):
        sent_first = jnp.int32(0)
        got_first = jnp.int32(0)
        for other in range(peers):
            sent_first = sent_first + jnp.where(other < s, plan_smem[0, source, other], 0)
            if other < source:
                got_first = got_first + plan_smem[0, other, s]
        number = plan_smem[0, source, s]
        for k in range(tokens // LANES):
            rank = lane + k * LANES - sent_first
            inside = (rank >= 0) & (rank < number)
            position = jnp.where(inside, rank + got_first, -1)
            value = (flat[source, k : k + 1, :] + source * block_rows).astype(F32)
            total = total + jnp.where(places == position, value, 0.0)
    index = jnp.sum(total, axis=1, keepdims=True).astype(jnp.int32)

    lax.fori_loop(0, (peers - 1) * tables, second, 0)

    def arrived(i, carry):
        source = i // tables
        o = lax.rem(i, tables)
        place = rows.at[source, 1 - c, o]
        remote(place, place, ssend.at[source, o], srecv.at[source, o], sib).wait_recv()
        return carry

    lax.fori_loop(0, peers * tables, arrived, 0)

    hidden = jnp.zeros((mine, width), F32)
    for source in range(peers):
        picks = jnp.where(index == iota((1, block_rows), 1) + source * block_rows, 1.0, 0.0).astype(BF16)
        hidden = hidden + jnp.dot(
            picks, rows[source].reshape(block_rows, width), preferred_element_type=F32
        )

    wp_send.wait_recv()
    wo_send.wait_recv()

    out_copy = remote(
        made.at[1 - c], out_ref.at[0, pl.ds(c * mine, mine)], osend.at[0], orecv.at[0], sib
    )
    for layer in range(2):
        normed = (normalise(hidden) * par[layer, 4:5, :]).astype(BF16)
        parts = []
        for k in range(4):
            projected = jnp.dot(
                normed, wp[layer, :, k * width : (k + 1) * width], preferred_element_type=F32
            )
            parts.append(silu_of_half(projected * 0.5 + par[layer, k : k + 1, :]).astype(BF16))
        gate, value, query, key = parts
        scale = 0.5 * head_size ** (-0.5)
        contract = (((1,), (1,)), ((), ()))
        batches = []
        for m in range(micro):
            r0, r1, r2 = m * MB_TOK, m * MB_TOK + lower, (m + 1) * MB_TOK
            heads = []
            for head in range(HEADS):
                f0, f1 = head * head_size, (head + 1) * head_size
                k_all = key[r0:r2, f0:f1]
                v_all = value[r0:r2, f0:f1]
                top = lax.dot_general(
                    query[r0:r1, f0:f1], k_all[:lower], contract, preferred_element_type=F32
                )
                low = lax.dot_general(query[r1:r2, f0:f1], k_all, contract, preferred_element_type=F32)
                top = silu_of_half(top * scale + grid[layer, head, :, lower:])
                low = silu_of_half(low * scale + grid[layer, head])
                top = (top * mask[m, :, 0:lower]).astype(BF16)
                low = (low * mask[m, :, lower:]).astype(BF16)
                heads.append(
                    jnp.concatenate(
                        [
                            jnp.dot(top, v_all[:lower], preferred_element_type=F32),
                            jnp.dot(low, v_all, preferred_element_type=F32),
                        ],
                        axis=0,
                    )
                )
            batches.append(jnp.concatenate(heads, axis=1))
        attended = jnp.concatenate(batches, axis=0)
        gated = (normalise(attended) * par[layer, 5:6, :] * gate.astype(F32)).astype(BF16)
        state = (hidden + jnp.dot(gated, wo[layer], preferred_element_type=F32)).astype(BF16)
        hidden = state.astype(F32)

        @pl.when(c == layer)
        def _():
            out_ref[0, pl.ds(pl.multiple_of(c * mine, mine), mine), :] = state

        @pl.when(c != layer)
        def _():
            made[layer] = state
            out_copy.start()

    def sent_table(k, carry):
        ask(k).wait_send()
        serve(k).wait_send()
        return carry

    def sent_seq(k, carry):
        tell(k).wait_send()
        return carry

    def sent_across(i, carry):
        across(1 + i // tables, lax.rem(i, tables)).wait_send()
        return carry

    def sent_beside(i, carry):
        beside(i // tables, lax.rem(i, tables)).wait_send()
        return carry

    lax.fori_loop(1, tables, sent_table, 0)
    lax.fori_loop(1, peers, sent_seq, 0)
    lax.fori_loop(0, (peers - 1) * tables, sent_across, 0)
    lax.fori_loop(0, peers * tables, sent_beside, 0)
    par_copy.wait_send()
    wp_send.wait_send()
    wo_send.wait_send()
    out_copy.wait()


def shards(
    table_slab,
    request_rows,
    owner_counts,
    item_slots,
    regroup_counts,
    history_lengths,
    w_proj,
    bias_proj,
    gain_in,
    gain_mid,
    rel_bias,
    w_out,
):
    peers = lax.axis_size("seq")
    tables = lax.axis_size("table")
    slab_rows, width = table_slab.shape
    tokens = item_slots.shape[1]
    half = CAP // 2
    msg_rows = (request_rows.shape[1] // LANES + 1 + 7) // 8 * 8
    micro = tokens // 2 // MB_TOK
    vmem = pl.BlockSpec(memory_space=pltpu.VMEM)
    smem = pl.BlockSpec(memory_space=pltpu.SMEM)
    hbm = pl.BlockSpec(memory_space=pl.ANY)
    dma = pltpu.SemaphoreType.DMA
    return pl.pallas_call(
        functools.partial(kernel, (peers, tables)),
        out_shape=jax.ShapeDtypeStruct((1, tokens, width), BF16),
        in_specs=[hbm, vmem, smem, vmem, smem, smem, hbm, vmem, vmem, vmem, vmem, hbm],
        out_specs=vmem,
        scratch_shapes=[
            pltpu.VMEM((slab_rows, width), BF16),
            pltpu.VMEM((2, width, 4 * width), BF16),
            pltpu.VMEM((2, width, width), BF16),
            pltpu.VMEM((2, 16, width), F32),
            pltpu.VMEM((tables, msg_rows, LANES), jnp.int32),
            pltpu.VMEM((peers, tokens // LANES, LANES), jnp.int32),
            pltpu.VMEM((tables, half, LANES), jnp.int32),
            pltpu.VMEM((tables, half, width), BF16),
            pltpu.VMEM((peers, 2, tables, half, width), BF16),
            pltpu.VMEM((2, HEADS, LANES, 2 * LANES), F32),
            pltpu.VMEM((micro, MB_TOK // 2, MB_TOK + MB_TOK // 2), F32),
            pltpu.VMEM((2, tokens // 2, width), BF16),
            dma((3,)),
            dma((3,)),
            dma((3,)),
            dma((tables,)),
            dma((tables,)),
            dma((peers,)),
            dma((peers,)),
            dma((tables,)),
            dma((tables,)),
            dma((peers, tables)),
            dma((peers, tables)),
            dma((peers, tables)),
            dma((peers, tables)),
            dma((1,)),
            dma((1,)),
        ],
        compiler_params=pltpu.CompilerParams(
            collective_id=0, has_side_effects=True, vmem_limit_bytes=48 * 1024 * 1024
        ),
        name="hstu_window",
    )(
        table_slab,
        request_rows,
        owner_counts,
        item_slots,
        regroup_counts,
        history_lengths,
        w_proj,
        bias_proj,
        gain_in,
        gain_mid,
        rel_bias,
        w_out,
    )


def solution(mesh):
    in_specs = (
        P("table", None),
        P(("seq", "table"), None),
        P(("seq", "table"), None),
        P(("seq", "table"), None),
        P("table", None, None),
        P(("seq", "table"), None),
        P("section", None, None),
        P("section", None),
        P("section", None),
        P("section", None),
        P("section", None, None),
        P("section", None, None),
    )
    out_specs = P("section", ("seq", "table"), None)
    return jax.shard_map(shards, mesh=mesh, in_specs=in_specs, out_specs=out_specs, check_vma=False)
```

time: 158 us -> 43.9 us (0.28)
  the two profiles are of different devices: /device:TPU:0 before, /device:TPU:13 now
where the time goes in v2:
time: 43.9 us; the launch traced here: 43.5 us
  Pallas kernels  32.5 us (74%)
  local copies, waits for them, and re-layouts  10.9 us (25%)
    pallas_call x1, Pallas kernels, shards(): pl.pallas_call(functools.partial(kernel, (peers, tables)), out_shape=jax....  32.5 us
    unnamed x25, local copies, waits for them, and re-layouts  10.9 us

profile of v2, /device:TPU:13, one launch (start us, length us, event | category | flops | bytes accessed | tf_op | source)
XLA Modules:
  0.0 43.5 jit_solution(8351857763861849577)
XLA Ops:
  0.0 0.0 copy-start
  0.0 1.6 %copy-done = bf16[1,512,2048]{2,1,0:T(8,128)(2,1)S(1)} copy-done((bf16[1,512,2048]{2,1,0:T(8,128)(2,1)S(1)}, bf16[1,512,2048]{2,1,0:T(8,128)(2,1)}, u32[]{:S(2)}) %copy-start) | copy-done | bytes 2097176
  1.6 1.2 %copy-done.1 = bf16[1024,512]{1,0:T(8,128)(2,1)S(1)} copy-done((bf16[1024,512]{1,0:T(8,128)(2,1)S(1)}, bf16[1024,512]{1,0:T(8,128)(2,1)}, u32[]{:S(2)}) %copy-start.1) | copy-done | bytes 1048600
  2.8 0.0 copy-start.2
  2.8 1.0 %copy-done.2 = bf16[1,512,512]{2,1,0:T(8,128)(2,1)S(1)} copy-done((bf16[1,512,512]{2,1,0:T(8,128)(2,1)S(1)}, bf16[1,512,512]{2,1,0:T(8,128)(2,1)}, u32[]{:S(2)}) %copy-start.2) | copy-done | bytes 524312
  3.9 0.0 copy-start.3
  3.9 0.7 %copy-done.3 = f32[1,2048]{1,0:T(1,128)S(1)} copy-done((f32[1,2048]{1,0:T(1,128)S(1)}, f32[1,2048]{1,0:T(1,128)}, u32[]{:S(2)}) %copy-start.3) | copy-done | bytes 8216
  4.6 0.0 copy-start.4
  4.6 0.7 %copy-done.4 = s32[1,1024]{1,0:T(1,128)S(1)} copy-done((s32[1,1024]{1,0:T(1,128)S(1)}, s32[1,1024]{1,0:T(1,128)}, u32[]{:S(2)}) %copy-start.4) | copy-done | bytes 4120
  5.2 0.0 copy-start.5
  5.2 0.7 %copy-done.5 = s32[1,512]{1,0:T(1,128)S(1)} copy-done((s32[1,512]{1,0:T(1,128)S(1)}, s32[1,512]{1,0:T(1,128)}, u32[]{:S(2)}) %copy-start.5) | copy-done | bytes 2072
  5.9 0.0 copy-start.6
  5.9 0.7 %copy-done.6 = s32[4,8]{1,0:T(4,128)S(1)} copy-done((s32[4,8]{1,0:T(4,128)S(1)}, s32[4,8]{1,0:T(4,128)}, u32[]{:S(2)}) %copy-start.6) | copy-done | bytes 152
  6.6 0.0 copy-start.7
  6.6 0.7 %copy-done.7 = f32[1,512]{1,0:T(1,128)S(1)} copy-done((f32[1,512]{1,0:T(1,128)S(1)}, f32[1,512]{1,0:T(1,128)}, u32[]{:S(2)}) %copy-start.7) | copy-done | bytes 2072
  7.3 0.0 copy-start.8
  7.3 0.7 %copy-done.8 = f32[1,512]{1,0:T(1,128)S(1)} copy-done((f32[1,512]{1,0:T(1,128)S(1)}, f32[1,512]{1,0:T(1,128)}, u32[]{:S(2)}) %copy-start.8) | copy-done | bytes 2072
  8.0 0.0 copy-start.9
  8.0 0.7 %copy-done.9 = f32[1,4,128]{2,1,0:T(4,128)S(1)} copy-done((f32[1,4,128]{2,1,0:T(4,128)S(1)}, f32[1,4,128]{2,1,0:T(4,128)}, u32[]{:S(2)}) %copy-start.9) | copy-done | bytes 2072
  8.7 0.0 copy-start.10
  8.7 0.7 %copy-done.10 = s32[1,2,2]{2,1,0:T(2,128)S(1)} copy-done((s32[1,2,2]{2,1,0:T(2,128)S(1)}, s32[1,2,2]{2,1,0:T(2,128)}, u32[]{:S(2)}) %copy-start.10) | copy-done | bytes 40
  9.3 0.7 %copy-done.11 = s32[1,8]{1,0:T(1,128)S(1)} copy-done((s32[1,8]{1,0:T(1,128)S(1)}, s32[1,8]{1,0:T(1,128)}, u32[]{:S(2)}) %copy-start.11) | copy-done | bytes 56
  10.0 32.5 %hstu_window.1 = bf16[1,1024,512]{2,1,0:T(8,128)(2,1)S(1)} custom-call(bf16[1024,512]{1,0:T(8,128)(2,1)S(1)} %copy-done.1, s32[1,512]{1,0:T(1,128)S(1)} %copy-done.5, s32[1,8]{1,0:T(1,128)S(1)} %copy-done.11, s32[1,1024]{1,0:T(1,128)S(1)} %copy-done.4, s32[1,2,2]{2,1,0:T(2,128)S(1)} %copy-done.10, s32[4,8]{1,0:T(4,128)S(1)} %copy-done.6, ...), custom_call_target="tpu_custom_call" | custom-call | tf_op jit(solution)/shard_map/hstu_window/pallas_call | solution.py:446
  42.5 1.0 %copy.14 = bf16[1,1024,512]{2,1,0:T(8,128)(2,1)} copy(bf16[1,1024,512]{2,1,0:T(8,128)(2,1)S(1)} %hstu_window.1) | data formatting | bytes 2097152
  (2 shorter events, 0.0 us)
Async XLA Ops:
  0.0 1.6 %copy-start = (bf16[1,512,2048]{2,1,0:T(8,128)(2,1)S(1)}, bf16[1,512,2048]{2,1,0:T(8,128)(2,1)}, u32[]{:S(2)}) copy-start(bf16[1,512,2048]{2,1,0:T(8,128)(2,1)} %wp_hbm.1) | copy-start | bytes 6291460
  1.6 1.2 %copy-start.1 = (bf16[1024,512]{1,0:T(8,128)(2,1)S(1)}, bf16[1024,512]{1,0:T(8,128)(2,1)}, u32[]{:S(2)}) copy-start(bf16[1024,512]{1,0:T(8,128)(2,1)} %slab_hbm.1) | copy-start | bytes 3145732
  2.8 1.0 %copy-start.2 = (bf16[1,512,512]{2,1,0:T(8,128)(2,1)S(1)}, bf16[1,512,512]{2,1,0:T(8,128)(2,1)}, u32[]{:S(2)}) copy-start(bf16[1,512,512]{2,1,0:T(8,128)(2,1)} %wo_hbm.1) | copy-start | bytes 1572868
  3.9 0.7 %copy-start.3 = (f32[1,2048]{1,0:T(1,128)S(1)}, f32[1,2048]{1,0:T(1,128)}, u32[]{:S(2)}) copy-start(f32[1,2048]{1,0:T(1,128)} %bias_ref.1) | copy-start | bytes 24580
  4.6 0.7 %copy-start.4 = (s32[1,1024]{1,0:T(1,128)S(1)}, s32[1,1024]{1,0:T(1,128)}, u32[]{:S(2)}) copy-start(s32[1,1024]{1,0:T(1,128)} %slots_ref.1) | copy-start | bytes 12292
  5.2 0.7 %copy-start.5 = (s32[1,512]{1,0:T(1,128)S(1)}, s32[1,512]{1,0:T(1,128)}, u32[]{:S(2)}) copy-start(s32[1,512]{1,0:T(1,128)} %req_ref.1) | copy-start | bytes 6148
  5.9 0.7 %copy-start.6 = (s32[4,8]{1,0:T(4,128)S(1)}, s32[4,8]{1,0:T(4,128)}, u32[]{:S(2)}) copy-start(s32[4,8]{1,0:T(4,128)} %lengths_smem.1) | copy-start | bytes 388
  6.6 0.7 %copy-start.7 = (f32[1,512]{1,0:T(1,128)S(1)}, f32[1,512]{1,0:T(1,128)}, u32[]{:S(2)}) copy-start(f32[1,512]{1,0:T(1,128)} %gin_ref.1) | copy-start | bytes 6148
  7.3 0.7 %copy-start.8 = (f32[1,512]{1,0:T(1,128)S(1)}, f32[1,512]{1,0:T(1,128)}, u32[]{:S(2)}) copy-start(f32[1,512]{1,0:T(1,128)} %gmid_ref.1) | copy-start | bytes 6148
  8.0 0.7 %copy-start.9 = (f32[1,4,128]{2,1,0:T(4,128)S(1)}, f32[1,4,128]{2,1,0:T(4,128)}, u32[]{:S(2)}) copy-start(f32[1,4,128]{2,1,0:T(4,128)} %rel_ref.1) | copy-start | bytes 6148
  8.7 0.7 %copy-start.10 = (s32[1,2,2]{2,1,0:T(2,128)S(1)}, s32[1,2,2]{2,1,0:T(2,128)}, u32[]{:S(2)}) copy-start(s32[1,2,2]{2,1,0:T(2,128)} %plan_smem.1) | copy-start | bytes 52
  9.3 0.7 %copy-start.11 = (s32[1,8]{1,0:T(1,128)S(1)}, s32[1,8]{1,0:T(1,128)}, u32[]{:S(2)}) copy-start(s32[1,8]{1,0:T(1,128)} %counts_smem.1) | copy-start | bytes 100

commit v3 on v2

--- a/solution.py
+++ b/solution.py
@@ -33,18 +33,27 @@
 def kernel(
     dims,
     slab_hbm,
+    req_hbm,
+    counts_hbm,
+    slots_hbm,
+    plan_hbm,
+    lengths_hbm,
+    wp_hbm,
+    bias_hbm,
+    gin_hbm,
+    gmid_hbm,
+    rel_hbm,
+    wo_hbm,
+    out_ref,
     req_ref,
     counts_smem,
     slots_ref,
     plan_smem,
     lengths_smem,
-    wp_hbm,
     bias_ref,
     gin_ref,
     gmid_ref,
     rel_ref,
-    wo_hbm,
-    out_ref,
     slab,
     wp,
     wo,
@@ -91,7 +100,16 @@
     sib = (1 - c, s, t)
 
     def table_peer(k):
-        return lax.rem(t + k, tables)
+        if tables & (tables - 1):
+            return lax.rem(t + k, tables)
+        flipped = 0
+        bit = 1
+        while bit < tables:
+            own = lax.rem(t // bit, 2)
+            turn = lax.rem(k // bit, 2)
+            flipped = flipped + bit * (own + turn - 2 * own * turn)
+            bit = 2 * bit
+        return flipped
 
     def seq_peer(k):
         return lax.rem(s + k, peers)
@@ -106,6 +124,24 @@
             device_id_type=MESH,
         )
 
+    small = [
+        pltpu.make_async_copy(source, place, local_sem.at[3 + k])
+        for k, (source, place) in enumerate(
+            (
+                (counts_hbm, counts_smem),
+                (req_hbm, req_ref),
+                (slots_hbm, slots_ref),
+                (bias_hbm, bias_ref),
+                (gin_hbm, gin_ref),
+                (gmid_hbm, gmid_ref),
+                (rel_hbm, rel_ref),
+                (lengths_hbm, lengths_smem),
+                (plan_hbm, plan_smem),
+            )
+        )
+    ]
+    for copy in small:
+        copy.start()
     slab_copy = pltpu.make_async_copy(slab_hbm, slab, local_sem.at[0])
     wp_copy = pltpu.make_async_copy(wp_hbm.at[0], wp.at[c], local_sem.at[1])
     wo_copy = pltpu.make_async_copy(wo_hbm.at[0], wo.at[c], local_sem.at[2])
@@ -126,6 +162,9 @@
     lax.fori_loop(1, tables, greet_table, 0)
     lax.fori_loop(1, peers, greet_seq, 0)
     pl.semaphore_signal(barrier, inc=1, device_id=sib, device_id_type=MESH)
+
+    for copy in small:
+        copy.wait()
 
     for k in range(listed):
         msg[t, k : k + 1, :] = req_ref[0:1, k * LANES : (k + 1) * LANES]
@@ -339,6 +378,9 @@
 
     out_copy = remote(
         made.at[1 - c], out_ref.at[0, pl.ds(c * mine, mine)], osend.at[0], orecv.at[0], sib
+    )
+    own_copy = pltpu.make_async_copy(
+        made.at[c], out_ref.at[0, pl.ds(c * mine, mine)], local_sem.at[12]
     )
     for layer in range(2):
         normed = (normalise(hidden) * par[layer, 4:5, :]).astype(BF16)
@@ -382,13 +424,14 @@
         state = (hidden + jnp.dot(gated, wo[layer], preferred_element_type=F32)).astype(BF16)
         hidden = state.astype(F32)
 
+        made[layer] = state
+
         @pl.when(c == layer)
         def _():
-            out_ref[0, pl.ds(pl.multiple_of(c * mine, mine), mine), :] = state
+            own_copy.start()
 
         @pl.when(c != layer)
         def _():
-            made[layer] = state
             out_copy.start()
 
     def sent_table(k, carry):
@@ -415,6 +458,7 @@
     par_copy.wait_send()
     wp_send.wait_send()
     wo_send.wait_send()
+    own_copy.wait()
     out_copy.wait()
 
 
@@ -439,16 +483,23 @@
     half = CAP // 2
     msg_rows = (request_rows.shape[1] // LANES + 1 + 7) // 8 * 8
     micro = tokens // 2 // MB_TOK
-    vmem = pl.BlockSpec(memory_space=pltpu.VMEM)
-    smem = pl.BlockSpec(memory_space=pltpu.SMEM)
-    hbm = pl.BlockSpec(memory_space=pl.ANY)
+    hbm = pl.BlockSpec(memory_space=pltpu.HBM)
     dma = pltpu.SemaphoreType.DMA
     return pl.pallas_call(
         functools.partial(kernel, (peers, tables)),
         out_shape=jax.ShapeDtypeStruct((1, tokens, width), BF16),
-        in_specs=[hbm, vmem, smem, vmem, smem, smem, hbm, vmem, vmem, vmem, vmem, hbm],
-        out_specs=vmem,
+        in_specs=[hbm] * 12,
+        out_specs=hbm,
         scratch_shapes=[
+            pltpu.VMEM(request_rows.shape, jnp.int32),
+            pltpu.SMEM(owner_counts.shape, jnp.int32),
+            pltpu.VMEM(item_slots.shape, jnp.int32),
+            pltpu.SMEM(regroup_counts.shape, jnp.int32),
+            pltpu.SMEM(history_lengths.shape, jnp.int32),
+            pltpu.VMEM(bias_proj.shape, F32),
+            pltpu.VMEM(gain_in.shape, F32),
+            pltpu.VMEM(gain_mid.shape, F32),
+            pltpu.VMEM(rel_bias.shape, F32),
             pltpu.VMEM((slab_rows, width), BF16),
             pltpu.VMEM((2, width, 4 * width), BF16),
             pltpu.VMEM((2, width, width), BF16),
@@ -461,7 +512,7 @@
             pltpu.VMEM((2, HEADS, LANES, 2 * LANES), F32),
             pltpu.VMEM((micro, MB_TOK // 2, MB_TOK + MB_TOK // 2), F32),
             pltpu.VMEM((2, tokens // 2, width), BF16),
-            dma((3,)),
+            dma((13,)),
             dma((3,)),
             dma((3,)),
             dma((tables,)),
@@ -478,7 +529,7 @@
             dma((1,)),
         ],
         compiler_params=pltpu.CompilerParams(
-            collective_id=0, has_side_effects=True, vmem_limit_bytes=48 * 1024 * 1024
+            collective_id=0, has_side_effects=True, vmem_limit_bytes=58 * 1024 * 1024
         ),
         name="hstu_window",
     )(

time: 43.9 us -> 34.9 us (0.79)
  the two profiles are of different devices: /device:TPU:13 before, /device:TPU:0 now
where the time goes in v3:
time: 34.9 us; the launch traced here: 34.7 us
  Pallas kernels  32.4 us (93%)
  local copies, waits for them, and re-layouts  2.26 us (6%)
    pallas_call x1, Pallas kernels, shards(): pl.pallas_call(functools.partial(kernel, (peers, tables)), out_shape=jax....  32.4 us
    unnamed x1, local copies, waits for them, and re-layouts  2.26 us

profile of v3, /device:TPU:0, one launch (start us, length us, event | category | flops | bytes accessed | tf_op | source)
XLA Modules:
  0.0 34.7 jit_solution(6510669635414936011)
XLA Ops:
  0.0 32.4 %hstu_window.1 = bf16[1,1024,512]{2,1,0:T(8,128)(2,1)} custom-call(bf16[1024,512]{1,0:T(8,128)(2,1)} %slab_hbm.1, s32[1,512]{1,0:T(1,128)} %req_hbm.1, s32[1,8]{1,0:T(1,128)} %counts_hbm.1, s32[1,1024]{1,0:T(1,128)} %slots_hbm.1, s32[1,2,2]{2,1,0:T(2,128)} %plan_hbm.1, s32[4,8]{1,0:T(4,128)} %lengths_hbm.1, bf16[1,512,2048]{2,1,0:T(8,128)(2,1)} %wp_hbm.1, ...), custom_call_target="tpu_custom_call" | custom-call | tf_op jit(solution)/shard_map/hstu_window/pallas_call | solution.py:488
  32.5 2.3 %copy.14 = bf16[1,1024,512]{2,1,0:T(8,128)(2,1)} copy(bf16[1,1024,512]{2,1,0:T(8,128)(2,1)} %hstu_window.1) | data formatting | bytes 2097152

commit v4 on v3

--- a/solution.py
+++ b/solution.py
@@ -320,21 +320,26 @@
 
     lax.fori_loop(1, peers, heard, 0)
 
+    def second(k):
+        o = table_peer(k)
+
+        def one(i, carry):
+            source = seq_peer(i)
+            place = rows.at[source, c, o]
+            remote(place, place, xsend.at[i, o], xrecv.at[source, o], (c, source, t)).wait_recv()
+            beside(source, o).start()
+            return carry
+
+        lax.fori_loop(1, peers, one, 0)
+
     def collect(k, carry):
         o = table_peer(k)
         remote(gath.at[o], rows.at[s, c, o], rsend.at[k], rrecv.at[o], (c, s, o)).wait_recv()
         pass_on(o)
+        second(k - 1)
         return carry
 
     lax.fori_loop(1, tables, collect, 0)
-
-    def second(i, carry):
-        source = seq_peer(1 + i // tables)
-        o = table_peer(lax.rem(i, tables))
-        place = rows.at[source, c, o]
-        remote(place, place, xsend.at[1, o], xrecv.at[source, o], (c, source, t)).wait_recv()
-        beside(source, o).start()
-        return carry
 
     chunk = mine
     places = iota((chunk, LANES), 0) + c * mine
@@ -355,7 +360,7 @@
             total = total + jnp.where(places == position, value, 0.0)
     index = jnp.sum(total, axis=1, keepdims=True).astype(jnp.int32)
 
-    lax.fori_loop(0, (peers - 1) * tables, second, 0)
+    second(tables - 1)
 
     def arrived(i, carry):
         source = i // tables

time: 34.9 us -> 39.1 us (1.12)
  Pallas kernels: 32.4 us -> 36.7 us
    pallas_call x1, Pallas kernels: 32.4 us -> 36.7 us  [shards(): pl.pallas_call(functools.partial(kernel, (peers, tables)), out_shape=jax....]
where the time goes in v4:
time: 39.1 us; the launch traced here: 38.9 us
  Pallas kernels  36.7 us (94%)
  local copies, waits for them, and re-layouts  2.26 us (6%)
    pallas_call x1, Pallas kernels, shards(): pl.pallas_call(functools.partial(kernel, (peers, tables)), out_shape=jax....  36.7 us
    unnamed x1, local copies, waits for them, and re-layouts  2.26 us

profile of v4, /device:TPU:0, one launch (start us, length us, event | category | flops | bytes accessed | tf_op | source)
XLA Modules:
  0.0 38.9 jit_solution(13023995113075396696)
XLA Ops:
  0.0 36.7 %hstu_window.1 = bf16[1,1024,512]{2,1,0:T(8,128)(2,1)} custom-call(bf16[1024,512]{1,0:T(8,128)(2,1)} %slab_hbm.1, s32[1,512]{1,0:T(1,128)} %req_hbm.1, s32[1,8]{1,0:T(1,128)} %counts_hbm.1, s32[1,1024]{1,0:T(1,128)} %slots_hbm.1, s32[1,2,2]{2,1,0:T(2,128)} %plan_hbm.1, s32[4,8]{1,0:T(4,128)} %lengths_hbm.1, bf16[1,512,2048]{2,1,0:T(8,128)(2,1)} %wp_hbm.1, ...), custom_call_target="tpu_custom_call" | custom-call | tf_op jit(solution)/shard_map/hstu_window/pallas_call | solution.py:493
  36.7 2.3 %copy.14 = bf16[1,1024,512]{2,1,0:T(8,128)(2,1)} copy(bf16[1,1024,512]{2,1,0:T(8,128)(2,1)} %hstu_window.1) | data formatting | bytes 2097152
